TPU v7x, 256 devices: a whole 4x4x8 slice. The times are simulated.
256 devices in a mesh: dp: 32 (over y, z), proto: 8 (over x, core).
Axes of the slice: x: 4, y: 4, z: 8, core: 2. Of those that a mesh axis runs over, the one named last changes fastest.
Arguments:
- embed: bfloat16 [16384, 1024], P('dp'), may hold values from -3 to 3
- prototypes: bfloat16 [1024, 32768], P(None, 'proto'), may hold values from -2 to 2
- partner: int32 [16384], P('dp'), may hold values from 0 to 16383, as said below
Outputs:
- grad_embed: float32 [16384, 1024], P('dp', 'proto')
- grad_protos: float32 [1024, 32768], P('dp', 'proto')
- view_swapped_cost: float32 [16384], P('dp')
Inputs may be any that keep to these rules, and one draw needn't show every extreme that they name: partner(partner(i)) = i and partner(i) != i; partner(i) lies in the same aligned block of 512 rows as i.
All inputs are finite; a program needn't handle non-finite values.
Results may differ from a plain program's by a relative error of at most 0.0015.
Values sent between devices are 32-bit elements; how exact they have to be, the bound alone decides.
No kernel may reach another device: no remote copies, remote signals or barrier semaphores. Data moves between devices by JAX's collectives and lax.ppermute only.
A program may use at most 128 MiB of HBM per device.

v0:
```python
import jax
import jax.numpy as jnp
from jax import lax
from jax.sharding import PartitionSpec as P

SINK_ITERS = 3


code_eps = 0.05
sharpness_divisor = 0.1


def local(embed, prototypes, partner):
    highest = lax.Precision.HIGHEST
    raw_embed = embed.astype(jnp.float32)
    embed_scale = lax.rsqrt(jnp.sum(raw_embed * raw_embed, axis=1) + 1e-06)
    unit_embed = (raw_embed * embed_scale[:, None]).astype(jnp.bfloat16)
    raw_protos = prototypes.astype(jnp.float32)
    proto_scale = lax.rsqrt(jnp.sum(raw_protos * raw_protos, axis=0) + 1e-06)
    unit_protos = (raw_protos * proto_scale[None, :]).astype(jnp.bfloat16)
    cluster_score_matrix = jnp.dot(unit_embed, unit_protos, preferred_element_type=jnp.float32)
    similarity_matrix = jnp.exp(cluster_score_matrix / code_eps)
    local_rows = embed.shape[0]
    companion_view_position = partner - lax.axis_index("dp") * local_rows
    sample_factor = jnp.ones((local_rows,), jnp.float32)
    column_factor = jnp.ones((similarity_matrix.shape[1],), jnp.float32)
    row_part = jnp.zeros((local_rows,), jnp.float32)
    for sweep_index in range(SINK_ITERS):
        column_factor = 1.0 / lax.psum(
            jnp.dot(sample_factor, similarity_matrix, precision=highest), "dp"
        )
        row_part = jnp.dot(similarity_matrix, column_factor, precision=highest)
        if sweep_index + 1 < SINK_ITERS:
            sample_factor = 1.0 / lax.psum(row_part, "proto")
    companion_view_entries = (
        jnp.take(similarity_matrix, companion_view_position, axis=0) * column_factor[None, :]
    )
    exponentiated_scores = jnp.exp(cluster_score_matrix / sharpness_divisor)
    normalizer_share = jnp.sum(exponentiated_scores, axis=1)
    sample_factor = 1.0 / lax.psum(row_part, "proto")
    balanced_assignments = (
        companion_view_entries * jnp.take(sample_factor, companion_view_position)[:, None]
    )
    normalizer_total, mismatch_summand = lax.psum(
        (normalizer_share, jnp.sum(balanced_assignments * cluster_score_matrix, axis=1)), "proto"
    )
    view_swapped_cost = jnp.log(normalizer_total) - mismatch_summand / sharpness_divisor
    score_derivative = (
        (exponentiated_scores / normalizer_total[:, None] - balanced_assignments)
        / sharpness_divisor
    ).astype(jnp.bfloat16)
    grad_protos = lax.psum_scatter(
        lax.dot_general(
            unit_embed,
            score_derivative,
            (((0,), (0,)), ((), ())),
            preferred_element_type=jnp.float32,
        ),
        "dp",
        scatter_dimension=0,
        tiled=True,
    )
    embed_term = lax.dot_general(
        score_derivative, unit_protos, (((1,), (1,)), ((), ())), preferred_element_type=jnp.float32
    )
    col_width = embed.shape[1] // lax.axis_size("proto")
    cubed = embed_scale * embed_scale * embed_scale
    grad_share = lax.psum_scatter(embed_term, "proto", scatter_dimension=1, tiled=True)
    own_embed = lax.dynamic_slice_in_dim(
        raw_embed, lax.axis_index("proto") * col_width, col_width, 1
    )
    inner_sum = lax.psum(jnp.sum(own_embed * grad_share, axis=1), "proto")
    grad_embed = embed_scale[:, None] * grad_share - (cubed * inner_sum)[:, None] * own_embed
    return (grad_embed, grad_protos, view_swapped_cost)


def solution(mesh):
    placed = (P("dp", None), P(None, "proto"), P("dp"))
    return jax.shard_map(
        local,
        mesh=mesh,
        in_specs=placed,
        out_specs=(P("dp", "proto"), P("dp", "proto"), P("dp")),
        check_vma=False,
    )
```

profile of v0, /device:TPU:4, one launch (start us, length us, event | category | flops | bytes accessed | tf_op | source)
XLA Modules:
  0.0 871.1 jit_solution(4835438706952586473)
XLA Ops:
  7.2 0.0 copy-start.1
  7.2 0.0 copy-start.3
  7.2 0.0 reduce-scatter.3.cloned.1.call-start
  7.2 5.1 fusion
  12.4 0.0 copy-done.1
  12.4 0.3 multiply_reduce_fusion.1
  12.7 0.0 copy-done.3
  12.7 10.5 %multiply_exponential_fusion = (f32[512,4096]{1,0:T(8,128)}, f32[512,4096]{1,0:T(8,128)S(1)}) fusion(bf16[1024,4096]{1,0:T(8,128)(2,1)} %param.4, f32[4096]{0:T(1024)S(1)} %add_rsqrt_fusion, f32[512]{0:T(512)S(1)} %add_rsqrt_fusion.1, bf16[512,1024]{1,0:T(8,128)(2,1)S(1)} %copy-done.1), kind=kOutput, calls=%fused_computation.9 | convolution fusion | flops 4311220224 | bytes 26232832 | tf_op jit(solution)/shard_map/dot_general | solution.py:21
  23.3 0.0 copy-start
  23.3 3.2 copy-done
  26.5 4.7 fusion.9
  31.2 146.1 %psum.64 = f32[4096]{0:T(1024)S(1)} all-reduce(f32[4096]{0:T(1024)S(1)} %bitcast.23), channel_id=1, replica_groups=mesh['dp'=32,'proto'=8] {'dp'}, use_global_device_ids=true, to_apply=%region_4.0 | all-reduce | flops 4096 | bytes 32768 | tf_op jit(solution)/shard_map/psum | solution.py:29
  177.4 10.2 %fusion.16 = f32[1,512]{1,0:T(1,128)S(1)} fusion(f32[4096,1]{0,1:T(1,128)S(1)} %bitcast.19, f32[512,4096]{1,0:T(8,128)} %copy-done), kind=kOutput, calls=%fused_computation.41 | convolution fusion | flops 27262976 | bytes 8407040 | tf_op jit(solution)/shard_map/dot_general | solution.py:32
  187.5 10.2 %psum.65 = f32[512]{0:T(512)S(1)} all-reduce(f32[512]{0:T(512)S(1)} %bitcast.24), channel_id=1, replica_groups=mesh['dp'=32,'proto'=8] {'proto'}, use_global_device_ids=true, to_apply=%region_5.0 | all-reduce | flops 512 | bytes 4096 | tf_op jit(solution)/shard_map/psum | solution.py:34
  197.8 7.1 fusion.15
  204.8 137.7 %psum.66 = f32[4096]{0:T(1024)S(1)} all-reduce(f32[4096]{0:T(1024)S(1)} %bitcast.20), channel_id=1, replica_groups=mesh['dp'=32,'proto'=8] {'dp'}, use_global_device_ids=true, to_apply=%region_6.0 | all-reduce | flops 4096 | bytes 32768 | tf_op jit(solution)/shard_map/psum | solution.py:29
  342.5 10.2 %fusion.14 = f32[1,512]{1,0:T(1,128)S(1)} fusion(f32[4096,1]{0,1:T(1,128)S(1)} %bitcast.21, f32[512,4096]{1,0:T(8,128)} %copy-done), kind=kOutput, calls=%fused_computation.39 | convolution fusion | flops 27262976 | bytes 8407040 | tf_op jit(solution)/shard_map/dot_general | solution.py:32
  352.7 10.2 %psum.67 = f32[512]{0:T(512)S(1)} all-reduce(f32[512]{0:T(512)S(1)} %bitcast.26), channel_id=1, replica_groups=mesh['dp'=32,'proto'=8] {'proto'}, use_global_device_ids=true, to_apply=%region_7.8 | all-reduce | flops 512 | bytes 4096 | tf_op jit(solution)/shard_map/psum | solution.py:34
  362.9 7.1 fusion.13
  370.0 137.7 %psum.68 = f32[4096]{0:T(1024)S(1)} all-reduce(f32[4096]{0:T(1024)S(1)} %bitcast.22), channel_id=1, replica_groups=mesh['dp'=32,'proto'=8] {'dp'}, use_global_device_ids=true, to_apply=%region_8.9 | all-reduce | flops 4096 | bytes 32768 | tf_op jit(solution)/shard_map/psum | solution.py:29
  507.7 10.2 %fusion.12 = f32[1,512]{1,0:T(1,128)S(1)} fusion(f32[4096,1]{0,1:T(1,128)S(1)} %bitcast.18, f32[512,4096]{1,0:T(8,128)} %copy-done), kind=kOutput, calls=%fused_computation.37 | convolution fusion | flops 27262976 | bytes 8407040 | tf_op jit(solution)/shard_map/dot_general | solution.py:32
  517.8 11.3 %psum.69 = f32[512]{0:T(512)S(1)} all-reduce(f32[512]{0:T(512)S(1)} %bitcast.28), channel_id=1, replica_groups=mesh['dp'=32,'proto'=8] {'proto'}, use_global_device_ids=true, to_apply=%region_9.10 | all-reduce | flops 512 | bytes 4096 | tf_op jit(solution)/shard_map/psum | solution.py:40
  529.1 12.2 %gather_fusion = f32[512,4096]{1,0:T(8,128)} fusion(f32[512,4096]{1,0:T(8,128)} %get-tuple-element.9, s32[1024]{0:T(1024)S(1)} %pad_clamp_fusion), kind=kCustom, calls=%fused_computation | custom fusion | bytes 16779264 | tf_op jit(solution)/shard_map/jit(_take)/gather | solution.py:36
  541.3 3.5 gather_fusion.1
  544.9 7.6 multiply_reduce_fusion
  552.4 14.2 %psum.63 = f32[512]{0:T(512)S(1)} all-reduce(f32[512]{0:T(512)S(1)} %get-tuple-element.4), channel_id=1, replica_groups=mesh['dp'=32,'proto'=8] {'proto'}, use_global_device_ids=true, to_apply=%region_3.0 | all-reduce | flops 512 | bytes 4096 | tf_op jit(solution)/shard_map/psum | solution.py:44
  566.7 7.5 multiply_convert_fusion
  574.2 0.0 copy-start.2
  574.2 1.9 copy-done.2
  576.1 8.3 fusion.3
  584.4 0.0 reduce-scatter.3.cloned.1.call-update
  584.4 0.0 reduce-scatter.5.cloned.1.call-start
  584.5 10.5 %fusion.7 = f32[1024,4096]{1,0:T(8,128)} fusion(bf16[512,4096]{1,0:T(8,128)(2,1)} %copy-done.2, f32[512]{0:T(512)S(1)} %add_rsqrt_fusion.1, bf16[512,1024]{1,0:T(8,128)(2,1)S(1)} %copy-done.1), kind=kOutput, calls=%fused_computation.16 | convolution fusion | flops 4296540160 | bytes 22022144 | tf_op jit(solution)/shard_map/dot_general | solution.py:53
  595.0 0.0 reduce-scatter.5.cloned.1.call-update
  595.0 0.2 convert_element_type.15
  595.2 15.4 %reduce-scatter.3.cloned.1.call-done = f32[512,128]{1,0:T(8,128)} async-done(((f32[512,1024]{1,0:T(8,128)}), f32[512,128]{1,0:T(8,128)}) %reduce-scatter.3.cloned.1.call-update) | async-done | bytes 262160 | tf_op jit(solution)/shard_map/reduce_scatter | solution.py:68
  610.7 1.1 multiply_reduce_fusion.2
  611.8 12.2 %all-reduce = (f32[512]{0:T(512)S(1)}, f32[512]{0:T(512)S(1)}) all-reduce(f32[512]{0:T(512)S(1)} %multiply_reduce_fusion.2, f32[512]{0:T(512)S(1)} %get-tuple-element.3), channel_id=1, replica_groups=mesh['dp'=32,'proto'=8] {'proto'}, use_global_device_ids=true, to_apply=%region_12.13 | all-reduce | flops 1024 | bytes 8192 | tf_op jit(solution)/shard_map/psum | solution.py:72
  624.0 0.6 fusion.8
  624.6 1.9 multiply_subtract_fusion
  626.5 237.4 %reduce-scatter.5.cloned.1.call-done = f32[32,4096]{1,0:T(8,128)} async-done(((f32[1024,4096]{1,0:T(8,128)}), f32[32,4096]{1,0:T(8,128)}) %reduce-scatter.5.cloned.1.call-update) | async-done | bytes 524304 | tf_op jit(solution)/shard_map/reduce_scatter | solution.py:52
  (11 shorter events, 0.1 us)
Async XLA Ops:
  7.2 5.2 copy-start.1
  7.2 5.5 copy-start.3
  7.2 603.5 %reduce-scatter.3.cloned.1.call-start = ((), (), s32[]{:S(2)}) async-start(), calls=%async_computation.2 | async-start | bytes 2359296 | tf_op jit(solution)/shard_map/reduce_scatter | solution.py:68
  23.3 3.2 copy-start
  574.2 1.9 copy-start.2
  584.4 279.4 %reduce-scatter.5.cloned.1.call-start = ((), (), s32[]{:S(2)}) async-start(), calls=%async_computation.3 | async-start | bytes 17301504 | tf_op jit(solution)/shard_map/reduce_scatter | solution.py:52
Sparse Core Ops, SparseCore 0:
  584.5 26.1 reduce-scatter.2
  615.4 248.4 reduce-scatter.4
where the time goes:
time: 879 us; the launch traced here: 871 us
  blocking collectives  480 us (55%)
  waiting for transfers between devices  253 us (29%)
  matrix products  78.8 us (9%)
  other arithmetic  24.3 us (3%)
  local copies, waits for them, and re-layouts  20.8 us (2%)
  between operations  14.6 us (2%)
    psum x3, blocking collectives, local(): lax.psum(jnp.dot(sample_factor, similarity_matrix, precision=highest), 'dp')  421 us
    reduce_scatter x1, waiting for transfers between devices, local(): lax.psum_scatter(lax.dot_general(unit_embed, score_derivative, (((0,), (0...  237 us
    psum x3, blocking collectives, local(): sample_factor = 1.0 / lax.psum(row_part, 'proto')  31.7 us
    dot_general x3, matrix products, local(): row_part = jnp.dot(similarity_matrix, column_factor, precision=highest)  30.5 us
    dot_general x3, matrix products, local(): jnp.dot(sample_factor, similarity_matrix, precision=highest)  18.9 us
  transfers between devices with their start and end apart: 2, of which 2 were waited for; matrix products, arithmetic and copies ran while one was open for 2% of the time, Pallas kernels for 0%

commit v1 on v0

v1 whole, which is shorter than its diff:
```python
import functools

import jax
import jax.numpy as jnp
from jax import lax
from jax.experimental import pallas as pl
from jax.experimental.pallas import tpu as pltpu
from jax.sharding import PartitionSpec as P

SINK_ITERS = 3
NY, NZ, NX = 4, 8, 4
ROWS, COLS, D = 512, 4096, 1024
F32, BF16 = jnp.float32, jnp.bfloat16
MIB = 1 << 20


code_eps = 0.05
sharpness_divisor = 0.1


def dp_pairs(f):
    pairs = []
    for y in range(NY):
        for z in range(NZ):
            to_y, to_z = f(y, z)
            pairs.append((y * NZ + z, (to_y % NY) * NZ + to_z % NZ))
    return pairs


def proto_pairs(f):
    pairs = []
    for x in range(NX):
        for core in range(2):
            to_x, to_core = f(x, core)
            pairs.append((x * 2 + core, (to_x % NX) * 2 + to_core % 2))
    return pairs


def move_y(v, off):
    return lax.ppermute(v, "dp", dp_pairs(lambda y, z: (y + off, z)))


def move_z(v, off):
    return lax.ppermute(v, "dp", dp_pairs(lambda y, z: (y, z + off)))


def move_x(v, off):
    return lax.ppermute(v, "proto", proto_pairs(lambda x, c: (x + off, c)))


def move_core(v):
    return lax.ppermute(v, "proto", proto_pairs(lambda x, c: (x, c + 1)))


def sum_y(v):
    return (v + move_y(v, 2)) + (move_y(v, 1) + move_y(v, -1))


def sum_z(v):
    v = v + lax.ppermute(v, "dp", dp_pairs(lambda y, z: (y, z ^ 1)))
    return (v + move_z(v, 4)) + (move_z(v, 2) + move_z(v, -2))


def sum_x(v):
    return (v + move_x(v, 2)) + (move_x(v, 1) + move_x(v, -1))


def sum_core(v):
    return v + move_core(v)


def sum_dp(v):
    return sum_z(sum_y(v))


def sum_proto(v):
    return sum_x(sum_core(v))


def scores_kernel(embed_ref, protos_ref, affinity_ref, scores_ref, col_ref, unit_ref):
    @pl.when(pl.program_id(0) == 0)
    def _():
        raw = embed_ref[...].astype(F32)
        scale = lax.rsqrt(jnp.sum(raw * raw, axis=1, keepdims=True) + 1e-06)
        unit_ref[...] = (raw * scale).astype(BF16)

    raw = protos_ref[...].astype(F32)
    scale = lax.rsqrt(jnp.sum(raw * raw, axis=0, keepdims=True) + 1e-06)
    unit_protos = (raw * scale).astype(BF16)
    scores = jnp.dot(unit_ref[...], unit_protos, preferred_element_type=F32)
    affinity = jnp.exp(scores / code_eps)
    scores_ref[...] = scores
    width = scores.shape[1]
    at = pl.ds(pl.multiple_of(pl.program_id(0) * width, width), width)
    affinity_ref[:, at] = affinity
    col_ref[:, at] = jnp.sum(affinity, axis=0, keepdims=True)


def first_scores(embed, prototypes, block=512):
    return pl.pallas_call(
        scores_kernel,
        grid=(COLS // block,),
        in_specs=[
            pl.BlockSpec((ROWS, D), lambda j: (0, 0)),
            pl.BlockSpec((D, block), lambda j: (0, j)),
        ],
        out_specs=[
            pl.BlockSpec(memory_space=pltpu.VMEM),
            pl.BlockSpec((ROWS, block), lambda j: (0, j)),
            pl.BlockSpec(memory_space=pltpu.VMEM),
        ],
        out_shape=[
            pltpu.VMEM((ROWS, COLS), F32),
            jax.ShapeDtypeStruct((ROWS, COLS), F32),
            jax.ShapeDtypeStruct((1, COLS), F32),
        ],
        scratch_shapes=[pltpu.VMEM((ROWS, D), BF16)],
        compiler_params=pltpu.CompilerParams(vmem_limit_bytes=40 * MIB),
        cost_estimate=pl.CostEstimate(
            flops=2 * ROWS * COLS * D, bytes_accessed=18 * MIB, transcendentals=ROWS * COLS
        ),
        name="first_scores",
    )(embed, prototypes)


def row_kernel(affinity_ref, col_total_ref, row_ref):
    weight = 1.0 / col_total_ref[...]
    rows = 64
    parts = []
    for i in range(ROWS // rows):
        total = jnp.zeros((rows, 128), F32)
        for j in range(COLS // 128):
            total += affinity_ref[i * rows : (i + 1) * rows, j * 128 : (j + 1) * 128] * weight[
                :, j * 128 : (j + 1) * 128
            ]
        parts.append(total)
    row_ref[...] = jnp.sum(jnp.concatenate(parts, axis=0).T, axis=0, keepdims=True)


def row_sums(affinity, col_total):
    return pl.pallas_call(
        row_kernel,
        in_specs=[pl.BlockSpec(memory_space=pltpu.VMEM)] * 2,
        out_specs=pl.BlockSpec(memory_space=pltpu.VMEM),
        out_shape=jax.ShapeDtypeStruct((1, ROWS), F32),
        compiler_params=pltpu.CompilerParams(vmem_limit_bytes=24 * MIB),
        cost_estimate=pl.CostEstimate(
            flops=2 * ROWS * COLS, bytes_accessed=8 * MIB, transcendentals=0
        ),
        name="row_sums",
    )(pltpu.with_memory_space_constraint(affinity, pltpu.VMEM), col_total)


def col_kernel(affinity_ref, row_total_ref, col_ref, weight_ref):
    weight = 1.0 / row_total_ref[...]
    weight_ref[...] = jnp.broadcast_to(weight, (128, ROWS)).T
    for j in range(COLS // 128):
        col_ref[:, j * 128 : (j + 1) * 128] = jnp.sum(
            affinity_ref[:, j * 128 : (j + 1) * 128] * weight_ref[...], axis=0, keepdims=True
        )


def col_sums(affinity, row_total):
    return pl.pallas_call(
        col_kernel,
        in_specs=[pl.BlockSpec(memory_space=pltpu.VMEM)] * 2,
        out_specs=pl.BlockSpec(memory_space=pltpu.VMEM),
        out_shape=jax.ShapeDtypeStruct((1, COLS), F32),
        scratch_shapes=[pltpu.VMEM((ROWS, 128), F32)],
        compiler_params=pltpu.CompilerParams(vmem_limit_bytes=24 * MIB),
        cost_estimate=pl.CostEstimate(
            flops=2 * ROWS * COLS, bytes_accessed=8 * MIB, transcendentals=0
        ),
        name="col_sums",
    )(pltpu.with_memory_space_constraint(affinity, pltpu.VMEM), row_total)


def local(embed, prototypes, partner):
    affinity, scores, col_part = first_scores(embed, prototypes)
    col_total = row_total = row_part = None
    for sweep in range(SINK_ITERS):
        if sweep:
            col_part = col_sums(affinity, row_total)
        col_total = sum_dp(col_part)
        row_part = row_sums(affinity, col_total)
        row_total = sum_proto(row_part)

    raw_embed = embed.astype(F32)
    embed_scale = lax.rsqrt(jnp.sum(raw_embed * raw_embed, axis=1) + 1e-06)
    unit_embed = (raw_embed * embed_scale[:, None]).astype(BF16)
    raw_protos = prototypes.astype(F32)
    proto_scale = lax.rsqrt(jnp.sum(raw_protos * raw_protos, axis=0) + 1e-06)
    unit_protos = (raw_protos * proto_scale[None, :]).astype(BF16)
    mate = partner - lax.axis_index("dp") * ROWS
    column_factor = 1.0 / col_total
    sample_factor = 1.0 / row_total.reshape(ROWS)
    exponentiated = jnp.exp(scores / sharpness_divisor)
    targets = (
        jnp.take(affinity, mate, axis=0) * column_factor * jnp.take(sample_factor, mate)[:, None]
    )
    denominator, mismatch = lax.psum(
        (jnp.sum(exponentiated, axis=1), jnp.sum(targets * scores, axis=1)), "proto"
    )
    cost = jnp.log(denominator) - mismatch / sharpness_divisor
    grad_scores = (
        (exponentiated / denominator[:, None] - targets) / sharpness_divisor
    ).astype(BF16)
    grad_protos = lax.psum_scatter(
        lax.dot_general(
            unit_embed, grad_scores, (((0,), (0,)), ((), ())), preferred_element_type=F32
        ),
        "dp",
        scatter_dimension=0,
        tiled=True,
    )
    embed_term = lax.dot_general(
        grad_scores, unit_protos, (((1,), (1,)), ((), ())), preferred_element_type=F32
    )
    inner = jnp.sum(raw_embed * embed_term, axis=1)
    cubed = embed_scale * embed_scale * embed_scale
    grad_embed = lax.psum_scatter(
        embed_scale[:, None] * embed_term - (cubed * inner)[:, None] * raw_embed,
        "proto",
        scatter_dimension=1,
        tiled=True,
    )
    return (grad_embed, grad_protos, cost)


def solution(mesh):
    placed = (P("dp", None), P(None, "proto"), P("dp"))
    return jax.shard_map(
        local,
        mesh=mesh,
        in_specs=placed,
        out_specs=(P("dp", "proto"), P("dp", "proto"), P("dp")),
        check_vma=False,
    )
```

time: 879 us -> 470 us (0.53)
  blocking collectives: 480 us -> 11.2 us
  matrix products: 78.8 us -> 19.3 us
  starting transfers between devices: 0.08 us -> 55.4 us
  waiting for transfers between devices: 253 us -> 305 us
  Pallas kernels: 0 us -> 15.3 us
    psum x8 -> x1, blocking collectives: 480 us -> 11.2 us  [local(): lax.psum((jnp.sum(exponentiated, axis=1), jnp.sum(targets * scores, axis=...]
    dot_general x9 -> x2, matrix products: 78.8 us -> 19.3 us  [the longest x1 10.4 us: local(): lax.dot_general(unit_embed, grad_scores, (((0,), (0,)), ((), ())), prefer...]
    ppermute x0 -> x33, starting transfers between devices: none -> 55.3 us  [the longest x9 23.2 us: move_z(): return lax.ppermute(v, 'dp', dp_pairs(lambda y, z: (y, z + off)))]
    ppermute x0 -> x33, waiting for transfers between devices: none -> 31.5 us  [the longest x9 9.74 us: move_z(): return lax.ppermute(v, 'dp', dp_pairs(lambda y, z: (y, z + off)))]
    reduce_scatter x2, waiting for transfers between devices: 253 us -> 274 us  [the longest x1 254 us: local(): lax.psum_scatter(lax.dot_general(unit_embed, grad_scores, (((0,), (0,)),...]
    pallas_call x0 -> x6, Pallas kernels: none -> 15.3 us  [the longest x1 11.8 us: first_scores(): pl.pallas_call(scores_kernel, grid=(COLS // block,), in_specs=[pl.BlockSp...]
  transfers between devices with their start and end apart: 2 -> 35, of which waited for: 2 -> 28; matrix products, arithmetic and copies ran while one was open for 2% -> 5% of each run, Pallas kernels for 0% -> 0%
where the time goes in v1:
time: 470 us; the launch traced here: 461 us
  waiting for transfers between devices  305 us (65%)
  starting transfers between devices  55.4 us (12%)
  local copies, waits for them, and re-layouts  20.3 us (4%)
  other arithmetic  19.4 us (4%)
  matrix products  19.3 us (4%)
  Pallas kernels  15.3 us (3%)
  between operations  14.7 us (3%)
  blocking collectives  11.2 us (2%)
    reduce_scatter x1, waiting for transfers between devices, local(): lax.psum_scatter(lax.dot_general(unit_embed, grad_scores, (((0,), (0,)),...  254 us
    ppermute x9, starting transfers between devices, move_z(): return lax.ppermute(v, 'dp', dp_pairs(lambda y, z: (y, z + off)))  23.2 us
    reduce_scatter x1, waiting for transfers between devices, local(): lax.psum_scatter(embed_scale[:, None] * embed_term - (cubed * inner)[:, N...  20.4 us
    ppermute x9, starting transfers between devices, move_y(): return lax.ppermute(v, 'dp', dp_pairs(lambda y, z: (y + off, z)))  15.4 us
    gather x1, local copies, waits for them, and re-layouts, local(): jnp.take(affinity, mate, axis=0) * column_factor  12.2 us
    ppermute x9, starting transfers between devices, move_x(): return lax.ppermute(v, 'proto', proto_pairs(lambda x, c: (x + off, c)))  12 us
    pallas_call x1, Pallas kernels, first_scores(): pl.pallas_call(scores_kernel, grid=(COLS // block,), in_specs=[pl.BlockSp...  11.8 us
    psum x1, blocking collectives, local(): lax.psum((jnp.sum(exponentiated, axis=1), jnp.sum(targets * scores, axis=...  11.2 us
  transfers between devices with their start and end apart: 35, of which 28 were waited for; matrix products, arithmetic and copies ran while one was open for 5% of the time, Pallas kernels for 0%

profile of v1, /device:TPU:4, one launch (start us, length us, event | category | flops | bytes accessed | tf_op | source)
XLA Modules:
  0.0 461.1 jit_solution(10875742907837601297)
XLA Ops:
  7.2 1.2 copy-done.2
  8.4 11.8 %first_scores.1 = (f32[512,4096]{1,0:T(8,128)S(1)}, f32[512,4096]{1,0:T(8,128)}, f32[1,4096]{1,0:T(1,128)S(1)}) custom-call(bf16[512,1024]{1,0:T(8,128)(2,1)S(1)} %copy-done.2, bf16[1024,4096]{1,0:T(8,128)(2,1)} %protos_ref.1), custom_call_target="tpu_custom_call" | custom-call | flops 4294967296 | bytes 18874368 | tf_op jit(solution)/shard_map/first_scores/pallas_call | solution.py:100
  20.3 3.2 collective-permute-start
  23.5 0.7 collective-permute-start.1
  24.1 2.6 collective-permute-start.2
  26.7 1.7 collective-permute-done.1
  28.4 2.0 collective-permute-start.3
  30.4 1.8 collective-permute-done.3
  32.3 7.3 %collective-permute-start.4 = (f32[1,4096]{1,0:T(1,128)S(1)}, f32[1,4096]{1,0:T(1,128)S(1)}, u32[]{:S(2)}, u32[]{:S(2)}) collective-permute-start(f32[1,4096]{1,0:T(1,128)S(1)} %add.149), channel_id=1, source_target_pairs={{0,32},{8,40},{16,48},{24,56},{32,0},{40,8},{48,16},{56,24},{64,96... | collective-permute-start | bytes 49160 | tf_op jit(solution)/shard_map/ppermute | solution.py:44
  39.6 1.5 collective-permute-start.5
  41.0 2.7 collective-permute-start.6
  43.7 1.7 collective-permute-done.5
  45.7 0.6 row_sums.3
  46.4 1.1 collective-permute-done.7
  48.1 2.7 collective-permute-start.8
  51.2 2.0 collective-permute-done.8
  53.2 1.2 collective-permute-done.9
  54.5 0.8 col_sums.2
  55.2 1.5 collective-permute-start.11
  56.8 2.6 collective-permute-start.12
  59.4 0.8 collective-permute-start.13
  60.6 1.2 collective-permute-done.12
  61.7 1.6 collective-permute-done.13
  63.3 1.5 collective-permute-start.14
  64.8 2.4 collective-permute-done.14
  67.2 2.3 collective-permute-start.15
  69.4 4.2 collective-permute-start.16
  73.6 1.3 collective-permute-done.15
  75.3 3.0 collective-permute-done.17
  79.0 1.1 collective-permute-done.18
  80.2 2.0 collective-permute-start.19
  82.5 1.7 collective-permute-start.21
  84.2 1.1 collective-permute-done.19
  85.7 0.7 collective-permute-done.21
  86.5 0.8 col_sums.3
  87.2 0.8 collective-permute-start.22
  88.0 1.9 collective-permute-start.23
  90.0 1.3 collective-permute-start.24
  91.3 1.3 collective-permute-done.22
  93.0 0.7 collective-permute-done.24
  93.8 1.1 collective-permute-start.25
  94.8 1.7 fusion
  96.5 1.1 collective-permute-done.25
  97.6 1.0 collective-permute-start.26
  98.6 2.9 collective-permute-start.27
  101.5 1.5 collective-permute-start.28
  103.0 2.4 collective-permute-done.26
  105.3 0.8 collective-permute-done.28
  106.2 3.4 copy-done.1
  109.5 0.6 row_sums.5
  110.3 1.1 collective-permute-done.29
  111.4 2.1 collective-permute-start.30
  113.5 1.5 collective-permute-start.31
  115.0 1.1 collective-permute-start.32
  116.1 12.2 %gather_fusion = f32[512,4096]{1,0:T(8,128)} fusion(f32[512,4096]{1,0:T(8,128)} %copy-done, s32[1024]{0:T(1024)S(1)} %pad_clamp_fusion), kind=kCustom, calls=%fused_computation | custom fusion | bytes 16779264 | tf_op jit(solution)/shard_map/jit(_take)/gather | solution.py:199
  128.4 3.5 gather_fusion.1
  131.9 7.6 %multiply_reduce_fusion = (f32[512]{0:T(512)S(1)}, f32[512]{0:T(512)S(1)}) fusion(f32[512,4096]{1,0:T(8,128)} %get-tuple-element.6, f32[512,4096]{1,0:T(8,128)} %gather_fusion, f32[512]{0:T(512)S(1)} %get-tuple-element.17, f32[4096]{0:T(1024)S(1)} %bitcast.7, pred[512]{0:T(512)(128)(4,1)S(1)} %get-tuple-element.18), kind=kLoop, calls=%fused_computation.7 | loop fusion | flops 14679040 | bytes 16800256 | tf_op jit(solution)/shard_map/reduce_sum | solution.py:202
  139.4 11.2 %all-reduce = (f32[512]{0:T(512)S(1)}, f32[512]{0:T(512)S(1)}) all-reduce(f32[512]{0:T(512)S(1)} %get-tuple-element.10, f32[512]{0:T(512)S(1)} %get-tuple-element.9), channel_id=1, replica_groups=mesh['dp'=32,'proto'=8] {'proto'}, use_global_device_ids=true, to_apply=%region_2.3 | all-reduce | flops 1024 | bytes 8192 | tf_op jit(solution)/shard_map/psum | solution.py:201
  150.7 7.5 %multiply_convert_fusion = bf16[512,4096]{1,0:T(8,128)(2,1)S(1)} fusion(f32[512,4096]{1,0:T(8,128)} %get-tuple-element.6, f32[512,4096]{1,0:T(8,128)} %gather_fusion, f32[512]{0:T(512)S(1)} %get-tuple-element.17, f32[4096]{0:T(1024)S(1)} %bitcast.8, f32[512]{0:T(512)S(1)} %get-tuple-element.13, pred[512]{0:T(512)(128)(4,1)S(1)} %get-tuple-element.18), kind=kLoop, calls=%fused_computation.9 | loop fusion | flops 16777216 | bytes 20992512 | tf_op jit(solution)/shard_map/convert_element_type | solution.py:207
  158.2 8.9 %fusion.6 = (f32[512]{0:T(512)S(1)}, f32[512]{0:T(512)S(1)}, f32[512,1024]{1,0:T(8,128)S(1)}) fusion(bf16[512,1024]{1,0:T(8,128)(2,1)S(1)} %copy-done.3, bf16[512,4096]{1,0:T(8,128)(2,1)S(1)} %multiply_convert_fusion, bf16[1024,4096]{1,0:T(8,128)(2,1)} %protos_ref.1, f32[4096]{0:T(1024)S(1)} %add_rsqrt_fusion), kind=kOutput, calls=%fused_computation.17 | convolution fusion | flops 4310170624 | bytes 15749120 | tf_op jit(solution)/shard_map/dot_general | solution.py:216
  167.2 1.7 fusion.8
  168.9 10.4 %fusion.10 = f32[1024,4096]{1,0:T(8,128)} fusion(bf16[512,4096]{1,0:T(8,128)(2,1)} %copy-done.4, bf16[512,1024]{1,0:T(8,128)(2,1)S(1)} %copy-done.3, f32[512]{0:T(512)S(1)} %get-tuple-element.19), kind=kOutput, calls=%fused_computation.21 | convolution fusion | flops 4296540160 | bytes 22022144 | tf_op jit(solution)/shard_map/dot_general | solution.py:209
  180.0 20.4 %reduce-scatter.3.cloned.1.call-done = f32[512,128]{1,0:T(8,128)} async-done(((f32[512,1024]{1,0:T(8,128)}), f32[512,128]{1,0:T(8,128)}) %reduce-scatter.3.cloned.1.call-update) | async-done | bytes 262160 | tf_op jit(solution)/shard_map/reduce_scatter | solution.py:221
  200.3 253.5 %reduce-scatter.5.cloned.1.call-done = f32[32,4096]{1,0:T(8,128)} async-done(((f32[1024,4096]{1,0:T(8,128)}), f32[32,4096]{1,0:T(8,128)}) %reduce-scatter.5.cloned.1.call-update) | async-done | bytes 524304 | tf_op jit(solution)/shard_map/reduce_scatter | solution.py:208
  (61 shorter events, 5.0 us)
Async XLA Ops:
  7.2 193.2 %reduce-scatter.3.cloned.1.call-start = ((), (), s32[]{:S(2)}) async-start(), calls=%async_computation.2 | async-start | bytes 2359296 | tf_op jit(solution)/shard_map/reduce_scatter | solution.py:221
  7.2 1.2 copy-start.2
  20.3 66.2 %copy-start = (f32[512,4096]{1,0:T(8,128)}, f32[512,4096]{1,0:T(8,128)S(1)}, u32[]{:S(2)}) copy-start(f32[512,4096]{1,0:T(8,128)S(1)} %get-tuple-element.7.affinity_ref) | copy-start | bytes 25165828
  20.3 6.4 %collective-permute-start = (f32[1,4096]{1,0:T(1,128)S(1)}, f32[1,4096]{1,0:T(1,128)S(1)}, u32[]{:S(2)}, u32[]{:S(2)}) collective-permute-start(f32[1,4096]{1,0:T(1,128)S(1)} %get-tuple-element.8), channel_id=1, source_target_pairs={{0,128},{8,136},{16,144},{24,152},{32,160},{40,168},{48,176},{56,1... | collective-permute-start | bytes 49160 | tf_op jit(solution)/shard_map/ppermute | solution.py:40
  23.5 4.9 %collective-permute-start.1 = (f32[1,4096]{1,0:T(1,128)S(1)}, f32[1,4096]{1,0:T(1,128)S(1)}, u32[]{:S(2)}, u32[]{:S(2)}) collective-permute-start(f32[1,4096]{1,0:T(1,128)S(1)} %get-tuple-element.8), channel_id=1, source_target_pairs={{0,64},{8,72},{16,80},{24,88},{32,96},{40,104},{48,112},{56,120},{... | collective-permute-start | bytes 49160 | tf_op jit(solution)/shard_map/ppermute | solution.py:40
  24.1 4.3 collective-permute-start.2
  28.4 3.8 collective-permute-start.3
  32.3 11.4 %collective-permute-start.4 = (f32[1,4096]{1,0:T(1,128)S(1)}, f32[1,4096]{1,0:T(1,128)S(1)}, u32[]{:S(2)}, u32[]{:S(2)}) collective-permute-start(f32[1,4096]{1,0:T(1,128)S(1)} %add.149), channel_id=1, source_target_pairs={{0,32},{8,40},{16,48},{24,56},{32,0},{40,8},{48,16},{56,24},{64,96... | collective-permute-start | bytes 49160 | tf_op jit(solution)/shard_map/ppermute | solution.py:44
  39.6 5.8 %collective-permute-start.5 = (f32[1,4096]{1,0:T(1,128)S(1)}, f32[1,4096]{1,0:T(1,128)S(1)}, u32[]{:S(2)}, u32[]{:S(2)}) collective-permute-start(f32[1,4096]{1,0:T(1,128)S(1)} %add.149), channel_id=1, source_target_pairs={{0,16},{8,24},{16,32},{24,40},{32,48},{40,56},{48,0},{56,8},{64,80... | collective-permute-start | bytes 49160 | tf_op jit(solution)/shard_map/ppermute | solution.py:44
  41.0 4.6 %collective-permute-start.6 = (f32[1,4096]{1,0:T(1,128)S(1)}, f32[1,4096]{1,0:T(1,128)S(1)}, u32[]{:S(2)}, u32[]{:S(2)}) collective-permute-start(f32[1,4096]{1,0:T(1,128)S(1)} %add.149), channel_id=1, source_target_pairs={{0,48},{8,56},{16,0},{24,8},{32,16},{40,24},{48,32},{56,40},{64,11... | collective-permute-start | bytes 49160 | tf_op jit(solution)/shard_map/ppermute | solution.py:44
  46.3 1.2 collective-permute-start.7
  47.6 3.6 collective-permute-start.10
  48.1 5.1 %collective-permute-start.8 = (f32[1,512]{1,0:T(1,128)S(1)}, f32[1,512]{1,0:T(1,128)S(1)}, u32[]{:S(2)}, u32[]{:S(2)}) collective-permute-start(f32[1,512]{1,0:T(1,128)S(1)} %add.153), channel_id=1, source_target_pairs={{0,4},{1,5},{2,6},{3,7},{4,0},{5,1},{6,2},{7,3},{8,12},{9,13},{10,... | collective-permute-start | bytes 6152 | tf_op jit(solution)/shard_map/ppermute | solution.py:48
  50.9 3.6 collective-permute-start.9
  55.2 5.3 %collective-permute-start.11 = (f32[1,4096]{1,0:T(1,128)S(1)}, f32[1,4096]{1,0:T(1,128)S(1)}, u32[]{:S(2)}, u32[]{:S(2)}) collective-permute-start(f32[1,4096]{1,0:T(1,128)S(1)} %col_sums.2), channel_id=1, source_target_pairs={{0,128},{8,136},{16,144},{24,152},{32,160},{40,168},{48,176},{56,1... | collective-permute-start | bytes 49160 | tf_op jit(solution)/shard_map/ppermute | solution.py:40
  56.8 4.9 %collective-permute-start.12 = (f32[1,4096]{1,0:T(1,128)S(1)}, f32[1,4096]{1,0:T(1,128)S(1)}, u32[]{:S(2)}, u32[]{:S(2)}) collective-permute-start(f32[1,4096]{1,0:T(1,128)S(1)} %col_sums.2), channel_id=1, source_target_pairs={{0,64},{8,72},{16,80},{24,88},{32,96},{40,104},{48,112},{56,120},{... | collective-permute-start | bytes 49160 | tf_op jit(solution)/shard_map/ppermute | solution.py:40
  59.4 3.9 collective-permute-start.13
  63.3 3.8 collective-permute-start.14
  67.2 7.8 %collective-permute-start.15 = (f32[1,4096]{1,0:T(1,128)S(1)}, f32[1,4096]{1,0:T(1,128)S(1)}, u32[]{:S(2)}, u32[]{:S(2)}) collective-permute-start(f32[1,4096]{1,0:T(1,128)S(1)} %add.160), channel_id=1, source_target_pairs={{0,32},{8,40},{16,48},{24,56},{32,0},{40,8},{48,16},{56,24},{64,96... | collective-permute-start | bytes 49160 | tf_op jit(solution)/shard_map/ppermute | solution.py:44
  69.4 5.8 %collective-permute-start.16 = (f32[1,4096]{1,0:T(1,128)S(1)}, f32[1,4096]{1,0:T(1,128)S(1)}, u32[]{:S(2)}, u32[]{:S(2)}) collective-permute-start(f32[1,4096]{1,0:T(1,128)S(1)} %add.160), channel_id=1, source_target_pairs={{0,16},{8,24},{16,32},{24,40},{32,48},{40,56},{48,0},{56,8},{64,80... | collective-permute-start | bytes 49160 | tf_op jit(solution)/shard_map/ppermute | solution.py:44
  73.6 4.6 %collective-permute-start.17 = (f32[1,4096]{1,0:T(1,128)S(1)}, f32[1,4096]{1,0:T(1,128)S(1)}, u32[]{:S(2)}, u32[]{:S(2)}) collective-permute-start(f32[1,4096]{1,0:T(1,128)S(1)} %add.160), channel_id=1, source_target_pairs={{0,48},{8,56},{16,0},{24,8},{32,16},{40,24},{48,32},{56,40},{64,11... | collective-permute-start | bytes 49160 | tf_op jit(solution)/shard_map/ppermute | solution.py:44
  78.3 16.5 %slice-start = ((s8[8388608]{0:T(1024)(128)(4,1)}), s8[4194304]{0:T(1024)(128)(4,1)S(1)}, s32[]{:S(2)}) async-start(s8[8388608]{0:T(1024)(128)(4,1)} %bitcast.5), calls=%async_computation.4 | async-start | bytes 8388608
  78.9 1.2 collective-permute-start.18
  80.2 5.1 %collective-permute-start.19 = (f32[1,512]{1,0:T(1,128)S(1)}, f32[1,512]{1,0:T(1,128)S(1)}, u32[]{:S(2)}, u32[]{:S(2)}) collective-permute-start(f32[1,512]{1,0:T(1,128)S(1)} %add.164), channel_id=1, source_target_pairs={{0,4},{1,5},{2,6},{3,7},{4,0},{5,1},{6,2},{7,3},{8,12},{9,13},{10,... | collective-permute-start | bytes 6152 | tf_op jit(solution)/shard_map/ppermute | solution.py:48
  82.1 3.6 collective-permute-start.20
  82.5 4.0 collective-permute-start.21
  86.5 8.4 %slice-start.1 = ((s8[8388608]{0:T(1024)(128)(4,1)}), s8[4194304]{0:T(1024)(128)(4,1)S(1)}, s32[]{:S(2)}) async-start(s8[8388608]{0:T(1024)(128)(4,1)} %bitcast.5), calls=%async_computation.5 | async-start | bytes 8388608
  87.2 5.3 %collective-permute-start.22 = (f32[1,4096]{1,0:T(1,128)S(1)}, f32[1,4096]{1,0:T(1,128)S(1)}, u32[]{:S(2)}, u32[]{:S(2)}) collective-permute-start(f32[1,4096]{1,0:T(1,128)S(1)} %col_sums.3), channel_id=1, source_target_pairs={{0,128},{8,136},{16,144},{24,152},{32,160},{40,168},{48,176},{56,1... | collective-permute-start | bytes 49160 | tf_op jit(solution)/shard_map/ppermute | solution.py:40
  88.0 4.9 %collective-permute-start.23 = (f32[1,4096]{1,0:T(1,128)S(1)}, f32[1,4096]{1,0:T(1,128)S(1)}, u32[]{:S(2)}, u32[]{:S(2)}) collective-permute-start(f32[1,4096]{1,0:T(1,128)S(1)} %col_sums.3), channel_id=1, source_target_pairs={{0,64},{8,72},{16,80},{24,88},{32,96},{40,104},{48,112},{56,120},{... | collective-permute-start | bytes 49160 | tf_op jit(solution)/shard_map/ppermute | solution.py:40
  90.0 3.7 collective-permute-start.24
  93.7 16.5 %copy-start.5 = (s32[512]{0:T(512)S(1)}, s32[512]{0:T(512)}, u32[]{:S(2)}) copy-start(s32[512]{0:T(512)} %param.5) | copy-start | bytes 6148
  93.8 3.8 collective-permute-start.25
  97.6 7.7 %collective-permute-start.26 = (f32[1,4096]{1,0:T(1,128)S(1)}, f32[1,4096]{1,0:T(1,128)S(1)}, u32[]{:S(2)}, u32[]{:S(2)}) collective-permute-start(f32[1,4096]{1,0:T(1,128)S(1)} %add.171), channel_id=1, source_target_pairs={{0,32},{8,40},{16,48},{24,56},{32,0},{40,8},{48,16},{56,24},{64,96... | collective-permute-start | bytes 49160 | tf_op jit(solution)/shard_map/ppermute | solution.py:44
  98.6 6.8 %collective-permute-start.27 = (f32[1,4096]{1,0:T(1,128)S(1)}, f32[1,4096]{1,0:T(1,128)S(1)}, u32[]{:S(2)}, u32[]{:S(2)}) collective-permute-start(f32[1,4096]{1,0:T(1,128)S(1)} %add.171), channel_id=1, source_target_pairs={{0,16},{8,24},{16,32},{24,40},{32,48},{40,56},{48,0},{56,8},{64,80... | collective-permute-start | bytes 49160 | tf_op jit(solution)/shard_map/ppermute | solution.py:44
  101.5 4.6 %collective-permute-start.28 = (f32[1,4096]{1,0:T(1,128)S(1)}, f32[1,4096]{1,0:T(1,128)S(1)}, u32[]{:S(2)}, u32[]{:S(2)}) collective-permute-start(f32[1,4096]{1,0:T(1,128)S(1)} %add.171), channel_id=1, source_target_pairs={{0,48},{8,56},{16,0},{24,8},{32,16},{40,24},{48,32},{56,40},{64,11... | collective-permute-start | bytes 49160 | tf_op jit(solution)/shard_map/ppermute | solution.py:44
  106.2 3.4 copy-start.1
  110.2 1.2 collective-permute-start.29
  111.4 16.9 %collective-permute-start.30 = (f32[1,512]{1,0:T(1,128)S(1)}, f32[1,512]{1,0:T(1,128)S(1)}, u32[]{:S(2)}, u32[]{:S(2)}) collective-permute-start(f32[1,512]{1,0:T(1,128)S(1)} %add.175), channel_id=1, source_target_pairs={{0,4},{1,5},{2,6},{3,7},{4,0},{5,1},{6,2},{7,3},{8,12},{9,13},{10,... | collective-permute-start | bytes 6152 | tf_op jit(solution)/shard_map/ppermute | solution.py:48
  113.5 14.8 %collective-permute-start.31 = (f32[1,512]{1,0:T(1,128)S(1)}, f32[1,512]{1,0:T(1,128)S(1)}, u32[]{:S(2)}, u32[]{:S(2)}) collective-permute-start(f32[1,512]{1,0:T(1,128)S(1)} %add.175), channel_id=1, source_target_pairs={{0,2},{1,3},{2,4},{3,5},{4,6},{5,7},{6,0},{7,1},{8,10},{9,11},{10,... | collective-permute-start | bytes 6152 | tf_op jit(solution)/shard_map/ppermute | solution.py:48
  115.0 13.3 %collective-permute-start.32 = (f32[1,512]{1,0:T(1,128)S(1)}, f32[1,512]{1,0:T(1,128)S(1)}, u32[]{:S(2)}, u32[]{:S(2)}) collective-permute-start(f32[1,512]{1,0:T(1,128)S(1)} %add.175), channel_id=1, source_target_pairs={{0,6},{1,7},{2,0},{3,1},{4,2},{5,3},{6,4},{7,5},{8,14},{9,15},{10,... | collective-permute-start | bytes 6152 | tf_op jit(solution)/shard_map/ppermute | solution.py:48
  150.6 7.5 %copy-start.3 = (bf16[512,1024]{1,0:T(8,128)(2,1)S(1)}, bf16[512,1024]{1,0:T(8,128)(2,1)}, u32[]{:S(2)}) copy-start(bf16[512,1024]{1,0:T(8,128)(2,1)} %embed_ref.1) | copy-start | bytes 3145732
  158.2 8.9 %copy-start.4 = (bf16[512,4096]{1,0:T(8,128)(2,1)}, bf16[512,4096]{1,0:T(8,128)(2,1)S(1)}, u32[]{:S(2)}) copy-start(bf16[512,4096]{1,0:T(8,128)(2,1)S(1)} %multiply_convert_fusion) | copy-start | bytes 12582916
  168.9 285.0 %reduce-scatter.5.cloned.1.call-start = ((), (), s32[]{:S(2)}) async-start(), calls=%async_computation.3 | async-start | bytes 17301504 | tf_op jit(solution)/shard_map/reduce_scatter | solution.py:208
Sparse Core Ops, SparseCore 0:
  169.0 31.2 reduce-scatter.2
  205.0 248.7 reduce-scatter.4
